TPU v7x, 32 devices: a whole 2x2x4 slice. The times are simulated.
32 devices in a mesh: leaf: 16 (over z, y, core), node: 2 (over x).
Axes of the slice: x: 2, y: 2, z: 4, core: 2. Of those that a mesh axis runs over, the one named last changes fastest.
Arguments:
- leaf_rhs: bfloat16 [16, 2048, 128], P('leaf', 'node'), may hold values from -6 to 6
- leaf_inverse: bfloat16 [16, 2048, 8192], P('leaf', 'node'), as said below
- leaf_update: bfloat16 [16, 1536, 2048], P('leaf', None, 'node'), may hold values from -0.0625 to 0.0625
- root_tiles: int32 [4, 12], replicated, may hold values from 0 to 23, all different within a row
- leaf_dinv: float32 [16, 2048], P('leaf', 'node'), may hold values from 0.5 to 2
- leaf_doff: float32 [16, 1024], P('leaf', 'node'), may hold values from -0.5 to 0.5
- leaf_pairs: int32 [16, 1024], P('leaf', 'node'), may hold values 0 or 1
- root_rhs: bfloat16 [3072, 128], P(('leaf', 'node')), may hold values from -6 to 6
- root_inverse: bfloat16 [3072, 3072], P(('leaf', 'node')), as said below
- root_dinv: float32 [3072], P(('leaf', 'node')), may hold values from 0.5 to 2
- root_doff: float32 [1536], P(('leaf', 'node')), may hold values from -0.5 to 0.5
- root_pairs: int32 [1536], P(('leaf', 'node')), may hold values 0 or 1
Outputs:
- leaf_solution: bfloat16 [16, 2048, 128], P('leaf', 'node')
- root_solution: bfloat16 [3072, 128], P(('leaf', 'node'))
Inputs may be any that keep to these rules, and one draw needn't show every extreme that they name: `leaf_inverse`: the 4 row blocks of each leaf, stacked, form Q M transpose(Q) for a permutation matrix Q and a unit lower triangular matrix M. root_inverse is unit lower triangular. `root_tiles`: the 12 tiles of one leaf are distinct, and every root tile is named by some leaf.
All inputs are finite; a program needn't handle non-finite values. No bound on the sum of `leaf_pairs` or of `root_pairs` on one device may be relied on, other than what follows from the above.
Results may differ from a plain program's by a relative error of at most 0.013.
Values may be sent and summed in bfloat16 or wider, within the bound.
A program may use at most 64 MiB of HBM per device.

v0:
```python
import jax
import jax.numpy as jnp
from jax import lax
from jax.sharding import PartitionSpec as P

LEAVES = 4
ROOT_TILES = 24


tile_rows = 128


def partner(value, axis, apart):
    mask = 2**apart
    pairs = [(source, source ^ mask) for source in range(lax.axis_size(axis))]
    return lax.ppermute(value, axis, pairs)


def pivot_solve(values, diagonal, coupling, pairs):
    length = values.shape[0]
    halves = values.reshape(length // 2, 2, values.shape[1])
    diag_two = diagonal.reshape(length // 2, 2)
    joined = (coupling * pairs.astype(jnp.float32))[:, None]
    first_row = diag_two[:, 0:1] * halves[:, 0, :] + joined * halves[:, 1, :]
    second_row = joined * halves[:, 0, :] + diag_two[:, 1:2] * halves[:, 1, :]
    return jnp.stack([first_row, second_row], axis=1).reshape(length, values.shape[1])


def transposed_product(matrix, vector):
    return lax.dot_general(
        matrix, vector, (((0,), (0,)), ((), ())), preferred_element_type=jnp.float32
    )


def on_device(
    leaf_rhs,
    leaf_inverse,
    leaf_update,
    root_tiles,
    leaf_dinv,
    leaf_doff,
    leaf_pairs,
    root_rhs,
    root_inverse,
    root_dinv,
    root_doff,
    root_pairs,
):
    factor_rows = leaf_inverse[0]
    local_rows = factor_rows.shape[0]
    rhs_count = leaf_rhs.shape[2]
    root_local = root_rhs.shape[0]
    group_size = lax.axis_size("leaf") // LEAVES
    node_count = lax.axis_size("node")
    bit_count = group_size.bit_length() - 1
    leaf_index = lax.axis_index("leaf")
    group_member = leaf_index % group_size
    leaf_owner = leaf_index // group_size
    block_rows = node_count * local_rows
    holding = lax.all_gather(leaf_rhs[0], "node", axis=0, tiled=True)
    block_start = group_member * block_rows
    own_columns = lax.dynamic_slice_in_dim(factor_rows, block_start, block_rows, 1)
    product_sum = jnp.dot(own_columns, holding, preferred_element_type=jnp.float32)
    for bit_number in range(bit_count):
        partner_rows = partner(holding, "leaf", bit_number)
        span_rows = holding.shape[0]
        partner_start = (group_member >> bit_number ^ 1) * span_rows
        columns = lax.dynamic_slice_in_dim(factor_rows, partner_start, span_rows, 1)
        product_sum = product_sum + jnp.dot(
            columns, partner_rows, preferred_element_type=jnp.float32
        )
        if bit_number + 1 < bit_count:
            low_side = group_member >> bit_number & 1 == 0
            holding = jnp.where(
                low_side,
                jnp.concatenate([holding, partner_rows], 0),
                jnp.concatenate([partner_rows, holding], 0),
            )
    leaf_forward = product_sum.astype(jnp.bfloat16)
    update_rows = leaf_update[0]
    tile_ids = lax.dynamic_index_in_dim(root_tiles, leaf_owner, 0, keepdims=False)
    tile_count = tile_ids.shape[0]
    onehot = (jnp.arange(ROOT_TILES, dtype=jnp.int32)[:, None] == tile_ids[None, :]).astype(
        jnp.float32
    )
    update_term = jnp.dot(update_rows, leaf_forward, preferred_element_type=jnp.float32)
    scattered = jnp.einsum(
        "tk,kar->tar",
        onehot,
        update_term.reshape(tile_count, tile_rows, rhs_count),
        precision=lax.Precision.HIGHEST,
    )
    scattered = scattered.reshape(ROOT_TILES * tile_rows, rhs_count)
    offset = lax.axis_index(("leaf", "node")) * root_local
    own_rows = lax.dynamic_update_slice_in_dim(
        jnp.zeros_like(scattered), root_rhs.astype(jnp.float32), offset, 0
    )
    merged = lax.psum(own_rows - scattered, ("leaf", "node")).astype(jnp.bfloat16)
    root_forward = jnp.dot(root_inverse, merged, preferred_element_type=jnp.float32)
    root_scaled = pivot_solve(root_forward, root_dinv, root_doff, root_pairs).astype(jnp.bfloat16)
    full_term = transposed_product(root_inverse, root_scaled)
    root_full = lax.psum(full_term, ("leaf", "node")).astype(jnp.bfloat16)
    own_offset = lax.axis_index(("leaf", "node")) * root_local
    root_own = lax.dynamic_slice_in_dim(root_full, own_offset, root_local, 0)
    tile_values = jnp.einsum(
        "tk,tar->kar",
        onehot.astype(jnp.bfloat16),
        root_full.reshape(ROOT_TILES, tile_rows, rhs_count),
        preferred_element_type=jnp.float32,
    )
    tile_values = tile_values.astype(jnp.bfloat16).reshape(tile_count * tile_rows, rhs_count)
    coupling_term = transposed_product(update_rows, tile_values)
    leaf_scaled = pivot_solve(
        leaf_forward.astype(jnp.float32), leaf_dinv[0], leaf_doff[0], leaf_pairs[0]
    )
    leaf_vector = (leaf_scaled - coupling_term).astype(jnp.bfloat16)
    back_term = transposed_product(factor_rows, leaf_vector)
    for bit_number in reversed(range(bit_count)):
        half_rows = back_term.shape[0] // 2
        lower_rows = back_term[:half_rows]
        upper_rows = back_term[half_rows:]
        high_side = group_member >> bit_number & 1 == 1
        outgoing = jnp.where(high_side, lower_rows, upper_rows)
        keeping = jnp.where(high_side, upper_rows, lower_rows)
        back_term = keeping + partner(outgoing.astype(jnp.bfloat16), "leaf", bit_number).astype(
            outgoing.dtype
        )
    leaf_solution = lax.psum_scatter(
        back_term.astype(jnp.bfloat16), "node", scatter_dimension=0, tiled=True
    )
    return (leaf_solution[None], root_own)


def solution(mesh):
    in_specs = (
        P("leaf", "node", None),
        P("leaf", "node", None),
        P("leaf", None, "node"),
        P(),
        P("leaf", "node"),
        P("leaf", "node"),
        P("leaf", "node"),
        P(("leaf", "node"), None),
        P(("leaf", "node"), None),
        P(("leaf", "node")),
        P(("leaf", "node")),
        P(("leaf", "node")),
    )
    out_specs = (P("leaf", "node", None), P(("leaf", "node"), None))
    return jax.shard_map(
        on_device, mesh=mesh, in_specs=in_specs, out_specs=out_specs, check_vma=False
    )
```

profile of v0, /device:TPU:0, one launch (start us, length us, event | category | flops | bytes accessed | tf_op | source)
XLA Modules:
  0.0 263.1 jit_solution(2733928216802699937)
XLA Ops:
  7.3 12.1 %all-gather = bf16[1,2048,128]{2,1,0:T(8,128)(2,1)} all-gather(bf16[1,1024,128]{2,1,0:T(8,128)(2,1)} %param.12), channel_id=2, replica_groups=mesh['leaf'=16,'node'=2] {'node'}, dimensions={1}, use_global_device_ids=true | all-gather | bytes 786432 | tf_op jit(solution)/shard_map/all_gather | solution.py:60
  20.7 1.3 reduce.11
  23.2 1.8 maximum_select_fusion
  25.0 1.6 collective-permute-start.1
  26.9 1.2 broadcast_in_dim.4
  28.8 3.6 %fusion.10 = f32[1024,128]{1,0:T(8,128)S(1)} fusion(bf16[1,1024,8192]{2,1,0:T(8,128)(2,1)} %param.13, s32[]{:T(128)S(6)} %select_n.63, bf16[1,2048,128]{2,1,0:T(8,128)(2,1)} %all-gather), kind=kOutput, calls=%fused_computation.8 | convolution fusion | flops 536870912 | bytes 5242884 | tf_op jit(solution)/shard_map/dot_general | solution.py:63
  32.4 18.3 %collective-permute-done.1 = bf16[4096,128]{1,0:T(8,128)(2,1)S(1)} collective-permute-done((bf16[4096,128]{1,0:T(8,128)(2,1)S(1)}, bf16[4096,128]{1,0:T(8,128)(2,1)S(1)}, u32[]{:S(2)}, u32[]{:S(2)}) %collective-permute-start.1) | collective-permute-done | bytes 1048608 | tf_op jit(solution)/shard_map/ppermute | solution.py:16
  50.6 5.7 %fusion.5 = f32[1024,128]{1,0:T(8,128)S(1)} fusion(bf16[4096,128]{1,0:T(8,128)(2,1)S(1)} %collective-permute-done.1, bf16[1,1024,8192]{2,1,0:T(8,128)(2,1)} %param.13, s32[]{:T(128)S(6)} %select_n.65), kind=kOutput, calls=%fused_computation.3 | convolution fusion | flops 1073741824 | bytes 9961476 | tf_op jit(solution)/shard_map/dot_general | solution.py:69
  56.3 3.6 %fusion.36 = bf16[1024,128]{1,0:T(8,128)(2,1)S(1)} fusion(f32[1024,128]{1,0:T(8,128)S(1)} %fusion.5, f32[1024,128]{1,0:T(8,128)S(1)} %fusion.10, bf16[2048,128]{1,0:T(8,128)(2,1)} %collective-permute-done, bf16[1,1024,8192]{2,1,0:T(8,128)(2,1)} %param.13, s32[]{:T(128)S(6)} %select_n.64), kind=kOutput, calls=%fused_computation.27 | convolution fusion | flops 537264128 | bytes 6029316 | tf_op jit(solution)/shard_map/dot_general | solution.py:69
  60.1 2.2 multiply_add_fusion.1
  62.3 1.3 pad_maximum_fusion
  63.6 2.0 copy.41
  65.6 2.0 fusion.18
  67.7 2.3 copy.33
  70.0 2.3 fusion.39
  72.6 2.7 %bitcast_subtract_fusion = f32[3072,128]{1,0:T(8,128)} fusion(f32[3072,128]{1,0:T(8,128)} %convert_dynamic-update-slice_fusion, f32[24,128,128]{2,1,0:T(8,128)S(1)} %copy.35), kind=kLoop, calls=%fused_computation.20 | loop fusion | flops 393216 | bytes 4718592 | tf_op jit(solution)/shard_map/sub | solution.py:98
  75.3 55.0 %all-reduce.2 = bf16[3072,128]{1,0:T(8,128)(2,1)} all-reduce(f32[3072,128]{1,0:T(8,128)} %bitcast_subtract_fusion), channel_id=1, replica_groups=mesh['leaf'=16,'node'=2] {'leaf','node'}, use_global_device_ids=true, to_apply=%region_0.1 | all-reduce | flops 393216 | bytes 2359296 | tf_op jit(solution)/shard_map/psum | solution.py:98
  130.3 1.6 fusion.57
  132.1 2.6 convolution_bitcast_fusion
  134.7 55.9 %all-reduce.3 = bf16[3072,128]{0,1:T(8,128)(2,1)} all-reduce(f32[3072,128]{0,1:T(8,128)} %convolution_bitcast_fusion), channel_id=1, replica_groups=mesh['leaf'=16,'node'=2] {'leaf','node'}, use_global_device_ids=true, to_apply=%region_1.2 | all-reduce | flops 393216 | bytes 2359296 | tf_op jit(solution)/shard_map/psum | solution.py:102
  190.7 2.2 copy.46
  192.8 2.6 %copy.39 = bf16[24,128,128]{2,0,1:T(8,128)(2,1)} copy(bf16[24,128,128]{1,0,2:T(8,128)(2,1)} %bitcast.90) | data formatting | bytes 1572864 | tf_op jit(solution)/shard_map/reshape | solution.py:108
  195.5 1.5 convolution_convert_fusion
  197.1 10.7 %fusion.2 = f32[8192,128]{0,1:T(8,128)} fusion(bf16[1,1024,8192]{2,1,0:T(8,128)(2,1)} %param.13, f32[1024,128]{0,1:T(8,128)} %copy.41, bf16[1536,128]{1,0:T(8,128)(2,1)S(1)} %bitcast.92, bf16[1,1536,1024]{2,1,0:T(8,128)(2,1)S(1)} %copy-done), kind=kOutput, calls=%fused_computation.2 | convolution fusion | flops 2550398976 | bytes 25034752 | tf_op jit(solution)/shard_map/dot_general | solution.py:30
  207.8 3.4 %select_convert_fusion = bf16[4096,128]{0,1:T(8,128)(2,1)} fusion(f32[8192,128]{0,1:T(8,128)} %fusion.2, pred[]{:T(512)S(6)} %eq.27), kind=kLoop, calls=%fused_computation.19 | loop fusion | flops 524288 | bytes 3145729 | tf_op jit(solution)/shard_map/convert_element_type | solution.py:125
  211.2 1.0 collective-permute-start.2
  212.2 22.8 %collective-permute-done.2 = bf16[4096,128]{0,1:T(8,128)(2,1)} collective-permute-done((bf16[4096,128]{0,1:T(8,128)(2,1)}, bf16[4096,128]{0,1:T(8,128)(2,1)}, u32[]{:S(2)}, u32[]{:S(2)}) %collective-permute-start.2) | collective-permute-done | bytes 1048608 | tf_op jit(solution)/shard_map/ppermute | solution.py:16
  235.0 2.9 %convert_add_fusion = f32[4096,128]{0,1:T(8,128)S(1)} fusion(bf16[4096,128]{0,1:T(8,128)(2,1)} %collective-permute-done.2, f32[8192,128]{0,1:T(8,128)} %fusion.2, pred[]{:T(512)S(6)} %eq.27), kind=kLoop, calls=%fused_computation.18 | loop fusion | flops 1572864 | bytes 7340033 | tf_op jit(solution)/shard_map/add | solution.py:125
  238.1 1.9 collective-permute-done.3
  240.0 1.0 add_convert_fusion
  242.7 11.8 %reduce-scatter.2.cloned.1.call-done = bf16[1024,128]{0,1:T(8,128)(2,1)} async-done(((bf16[2048,128]{0,1:T(8,128)(2,1)}), bf16[1024,128]{0,1:T(8,128)(2,1)}) %reduce-scatter.2.cloned.1.call-update) | async-done | bytes 262160 | tf_op jit(solution)/shard_map/reduce_scatter | solution.py:128
  254.4 1.8 copy.42
  (36 shorter events, 5.9 us)
Async XLA Ops:
  7.2 58.5 %copy-start = (bf16[1,1536,1024]{2,1,0:T(8,128)(2,1)S(1)}, bf16[1,1536,1024]{2,1,0:T(8,128)(2,1)}, u32[]{:S(2)}) copy-start(bf16[1,1536,1024]{2,1,0:T(8,128)(2,1)} %param.14) | copy-start | bytes 9437188
  7.2 19.7 %copy-start.5 = (s32[48]{0:T(128)S(1)}, s32[48]{0:T(128)}, u32[]{:S(2)}) copy-start(s32[48]{0:T(128)} %param.23) | copy-start | bytes 580
  7.2 19.7 %copy-start.4 = (f32[48]{0:T(128)S(1)}, f32[48]{0:T(128)}, u32[]{:S(2)}) copy-start(f32[48]{0:T(128)} %param.22) | copy-start | bytes 580
  7.2 19.7 %copy-start.3 = (s32[1,512]{1,0:T(1,128)S(1)}, s32[1,512]{1,0:T(1,128)}, u32[]{:S(2)}) copy-start(s32[1,512]{1,0:T(1,128)} %param.18) | copy-start | bytes 6148
  7.2 19.7 %copy-start.2 = (f32[1,512]{1,0:T(1,128)S(1)}, f32[1,512]{1,0:T(1,128)}, u32[]{:S(2)}) copy-start(f32[1,512]{1,0:T(1,128)} %param.17) | copy-start | bytes 6148
  7.2 21.0 %copy-start.1 = (bf16[96,128]{1,0:T(8,128)(2,1)S(1)}, bf16[96,128]{1,0:T(8,128)(2,1)}, u32[]{:S(2)}) copy-start(bf16[96,128]{1,0:T(8,128)(2,1)} %param.19) | copy-start | bytes 73732
  7.2 247.2 %reduce-scatter.2.cloned.1.call-start = ((), (), s32[]{:S(2)}) async-start(), calls=%async_computation.1 | async-start | bytes 786432 | tf_op jit(solution)/shard_map/reduce_scatter | solution.py:128
  19.4 3.7 %collective-permute-start = (bf16[2048,128]{1,0:T(8,128)(2,1)}, bf16[2048,128]{1,0:T(8,128)(2,1)}, u32[]{:S(2)}, u32[]{:S(2)}) collective-permute-start(bf16[2048,128]{1,0:T(8,128)(2,1)} %bitcast.1), channel_id=1, source_target_pairs={{0,2},{2,0},{4,6},{6,4},{8,10},{10,8},{12,14},{14,12},{16,18},{18,... | collective-permute-start | bytes 1572872 | tf_op jit(solution)/shard_map/ppermute | solution.py:16
  25.0 25.6 %collective-permute-start.1 = (bf16[4096,128]{1,0:T(8,128)(2,1)S(1)}, bf16[4096,128]{1,0:T(8,128)(2,1)S(1)}, u32[]{:S(2)}, u32[]{:S(2)}) collective-permute-start(bf16[4096,128]{1,0:T(8,128)(2,1)S(1)} %maximum_select_fusion), channel_id=1, source_target_pairs={{0,4},{2,6},{4,0},{6,2},{8,12},{10,14},{12,8},{14,10},{16,20},{18,... | collective-permute-start | bytes 3145736 | tf_op jit(solution)/shard_map/ppermute | solution.py:16
  211.2 23.8 %collective-permute-start.2 = (bf16[4096,128]{0,1:T(8,128)(2,1)}, bf16[4096,128]{0,1:T(8,128)(2,1)}, u32[]{:S(2)}, u32[]{:S(2)}) collective-permute-start(bf16[4096,128]{0,1:T(8,128)(2,1)} %select_convert_fusion), channel_id=1, source_target_pairs={{0,4},{2,6},{4,0},{6,2},{8,12},{10,14},{12,8},{14,10},{16,20},{18,... | collective-permute-start | bytes 3145736 | tf_op jit(solution)/shard_map/ppermute | solution.py:16
  238.0 2.0 collective-permute-start.3
Sparse Core Ops, SparseCore 0:
  241.1 13.2 reduce-scatter.1
where the time goes:
time: 264 us; the launch traced here: 263 us
  blocking collectives  123 us (47%)
  waiting for transfers between devices  54.7 us (21%)
  matrix products  33.7 us (13%)
  other arithmetic  17.7 us (7%)
  local copies, waits for them, and re-layouts  17 us (6%)
  between operations  14.3 us (5%)
  starting transfers between devices  2.67 us (1%)
    psum x1, blocking collectives, on_device(): root_full = lax.psum(full_term, ('leaf', 'node')).astype(jnp.bfloat16)  55.9 us
    psum x1, blocking collectives, on_device(): lax.psum(own_rows - scattered, ('leaf', 'node')).astype(jnp.bfloat16)  55 us
    ppermute x4, waiting for transfers between devices, partner(): return lax.ppermute(value, axis, pairs)  42.9 us
    dot_general x2, matrix products, transposed_product(): lax.dot_general(matrix, vector, (((0,), (0,)), ((), ())), preferred_eleme...  13.4 us
    all_gather x1, blocking collectives, on_device(): holding = lax.all_gather(leaf_rhs[0], 'node', axis=0, tiled=True)  12.1 us
    reduce_scatter x1, waiting for transfers between devices, on_device(): lax.psum_scatter(back_term.astype(jnp.bfloat16), 'node', scatter_dimensio...  11.8 us
    dot_general x2, matrix products, on_device(): jnp.dot(columns, partner_rows, preferred_element_type=jnp.float32)  9.28 us
  transfers between devices with their start and end apart: 5, of which 4 were waited for; matrix products, arithmetic and copies ran while one was open for 4% of the time, Pallas kernels for 0%

commit v1 on v0

--- a/solution.py
+++ b/solution.py
@@ -1,6 +1,10 @@
+import functools
+
 import jax
 import jax.numpy as jnp
 from jax import lax
+from jax.experimental import pallas as pl
+from jax.experimental.pallas import tpu as pltpu
 from jax.sharding import PartitionSpec as P
 
 LEAVES = 4
@@ -131,6 +135,511 @@
     return (leaf_solution[None], root_own)
 
 
+def flipped(value, mask):
+    bit = 1
+    while bit <= mask:
+        if mask & bit:
+            value = value + bit - 2 * bit * lax.rem(lax.div(value, bit), 2)
+        bit *= 2
+    return value
+
+
+def column_of(row, group):
+    count = row.shape[1]
+    length = -(-count * group // tile_rows) * tile_rows
+    shape = (length, count)
+    place = lax.broadcasted_iota(jnp.int32, shape, 0)
+    if group > 1:
+        place = lax.div(place, group)
+    lane = lax.broadcasted_iota(jnp.int32, shape, 1)
+    return jnp.sum(jnp.where(place == lane, row, 0.0), axis=1, keepdims=True)
+
+
+def paired(values, diagonal, joined):
+    length = values.shape[0]
+    odd = lax.rem(lax.broadcasted_iota(jnp.int32, values.shape, 0), 2) == 1
+    other = jnp.where(odd, pltpu.roll(values, 1, 0), pltpu.roll(values, length - 1, 0))
+    return diagonal * values + joined * other
+
+
+def solve_kernel(
+    leaves,
+    group_size,
+    node_count,
+    rhs_hbm,
+    inverse_hbm,
+    update_hbm,
+    tiles,
+    dinv,
+    doff,
+    pairs,
+    root_rhs,
+    root_inv_hbm,
+    root_dinv,
+    root_doff,
+    root_pairs,
+    leaf_out,
+    root_out,
+    right,
+    inverse,
+    update,
+    root_inv,
+    total,
+    forward,
+    term,
+    scaled_t,
+    vector_t,
+    values_t,
+    whole_t,
+    scattered,
+    near_out,
+    near_in,
+    far_out,
+    far_in,
+    deep_out,
+    deep_in,
+    reduced,
+    back_keep,
+    back_near_out,
+    back_near_in,
+    back_far_out,
+    back_far_in,
+    load_sem,
+    right_send,
+    right_recv,
+    sum_send,
+    sum_recv,
+    spread_send,
+    spread_recv,
+    back_send,
+    back_recv,
+):
+    f32, bf16 = jnp.float32, jnp.bfloat16
+    leaf = lax.axis_index("leaf")
+    node = lax.axis_index("node")
+    owner = lax.div(leaf, group_size)
+    member = lax.rem(leaf, group_size) * node_count + node
+    members = group_size * node_count
+    sib = node_count
+    cross = sorted((d for d in range(1, members) if not d & sib), key=lambda d: -bin(d).count("1"))
+    local = rhs_hbm.shape[1]
+    own_rows = root_rhs.shape[0]
+    band = members * own_rows
+    band_tiles = band // tile_rows
+    step = 2 * tile_rows
+    pending = []
+
+    def peer(d):
+        return flipped(leaf, d // node_count), flipped(node, d % node_count)
+
+    def level(dz):
+        other = lax.rem(owner + dz, leaves)
+        return other, (lax.rem(leaf + dz * group_size, leaves * group_size), node)
+
+    def send(source, target, send_sem, recv_sem, device):
+        copy = pltpu.make_async_remote_copy(
+            src_ref=source,
+            dst_ref=target,
+            send_sem=send_sem,
+            recv_sem=recv_sem,
+            device_id=device,
+            device_id_type=pl.DeviceIdType.MESH,
+        )
+        copy.start()
+        pending.append(copy)
+        return copy
+
+    order = [0, sib] + cross[::-1] + [d + sib for d in cross[::-1]]
+    loads = {}
+    for d in order:
+        start = pl.multiple_of(flipped(member, d) * local, tile_rows)
+        loads[d] = pltpu.make_async_copy(
+            inverse_hbm.at[0, :, pl.ds(start, local)], inverse.at[d], load_sem.at[d]
+        )
+    own_load = pltpu.make_async_copy(rhs_hbm.at[0], right.at[0], load_sem.at[members])
+    update_load = pltpu.make_async_copy(update_hbm.at[0], update, load_sem.at[members + 1])
+    root_load = pltpu.make_async_copy(
+        root_inv_hbm, root_inv.at[pl.ds(0, own_rows)], load_sem.at[members + 2]
+    )
+    own_load.start()
+    for d in order:
+        loads[d].start()
+    update_load.start()
+    root_load.start()
+
+    near = [sib] + cross
+    barrier = pltpu.get_barrier_semaphore()
+    for d in near:
+        pl.semaphore_signal(
+            barrier, inc=1, device_id=peer(d), device_id_type=pl.DeviceIdType.MESH
+        )
+    for dz in range(1, leaves):
+        pl.semaphore_signal(
+            barrier, inc=1, device_id=level(dz)[1], device_id_type=pl.DeviceIdType.MESH
+        )
+    pl.semaphore_wait(barrier, len(near) + leaves - 1)
+
+    arrivals = {}
+    for d in cross + [sib]:
+        arrivals[d] = send(
+            rhs_hbm.at[0], right.at[d], right_send.at[d], right_recv.at[d], peer(d)
+        )
+    total[...] = jnp.zeros_like(total)
+    if root_inv.shape[0] > own_rows:
+        root_inv[own_rows:, :] = jnp.zeros(
+            (root_inv.shape[0] - own_rows, root_inv.shape[1]), bf16
+        )
+
+    def product(d):
+        loads[d].wait()
+
+        @pl.loop(0, local // step)
+        def _(i):
+            rows = pl.ds(pl.multiple_of(i * step, step), step)
+            total[rows, :] += jnp.dot(
+                inverse[d, rows, :], right[d], preferred_element_type=f32
+            )
+
+    def relay(d):
+        arrivals[d].wait_recv()
+        arrivals[d + sib] = send(
+            right.at[d],
+            right.at[d + sib],
+            right_send.at[d + sib],
+            right_recv.at[d + sib],
+            peer(sib),
+        )
+
+    own_load.wait()
+    product(0)
+    arrivals[sib].wait_recv()
+    product(sib)
+    for d in cross[::-1][:-1]:
+        relay(d)
+    for d in cross[::-1][:-1]:
+        product(d)
+    relay(cross[0])
+    product(cross[0])
+    for d in cross[::-1]:
+        arrivals[d + sib].wait_recv()
+        product(d + sib)
+    forward[...] = total[...].astype(bf16)
+
+    update_load.wait()
+    tile_count = update.shape[0] // tile_rows
+
+    @pl.loop(0, tile_count)
+    def _(k):
+        rows = pl.ds(pl.multiple_of(k * tile_rows, tile_rows), tile_rows)
+        term[k] = jnp.dot(update[rows, :], forward[...], preferred_element_type=f32)
+
+    names = [tiles[owner, k] for k in range(tile_count)]
+    for t in range(leaves * band_tiles):
+        rows = pl.ds(t % band_tiles * tile_rows, tile_rows)
+        placed = jnp.zeros(term.shape[1:], f32)
+        for k in range(tile_count):
+            placed = jnp.where(names[k] == t, term[k], placed)
+        scattered[0, t // band_tiles, rows, :] = placed
+
+    def block_rows(d):
+        return pl.ds(pl.multiple_of(flipped(member, d) * own_rows, 16), own_rows)
+
+    spots = {d: i for i, d in enumerate(cross + [0])}
+
+    def sum_all(use, meanwhile):
+        first, second = {}, {}
+        for d in cross + [0]:
+            i = spots[d]
+            near_out[use, i] = scattered[use, :, block_rows(d + sib), :].astype(bf16)
+            first[d] = send(
+                near_out.at[use, i],
+                near_in.at[use, i],
+                sum_send.at[use, i],
+                sum_recv.at[use, i],
+                peer(sib),
+            )
+        base = len(spots)
+        for d in cross:
+            i = spots[d]
+            first[d].wait_recv()
+            both = scattered[use, :, block_rows(d), :] + near_in[use, i].astype(f32)
+            far_out[use, i] = both.astype(bf16)
+            second[d] = send(
+                far_out.at[use, i],
+                far_in.at[use, i],
+                sum_send.at[use, base + i],
+                sum_recv.at[use, base + i],
+                peer(d),
+            )
+        meanwhile()
+        first[0].wait_recv()
+        mine = scattered[use, :, block_rows(0), :] + near_in[use, spots[0]].astype(f32)
+        for d in cross:
+            second[d].wait_recv()
+            mine = mine + far_in[use, spots[d]].astype(f32)
+        deep_out[use] = mine.astype(bf16)
+        base += len(cross)
+        third = []
+        for dz in range(1, leaves):
+            other, device = level(dz)
+            third.append(
+                send(
+                    deep_out.at[use, other],
+                    deep_in.at[use, dz],
+                    sum_send.at[use, base + dz],
+                    sum_recv.at[use, base + dz],
+                    device,
+                )
+            )
+        result = deep_out[use, owner].astype(f32)
+        for dz in range(1, leaves):
+            third[dz - 1].wait_recv()
+            result = result + deep_in[use, dz].astype(f32)
+        return result
+
+    def spread(use, value):
+        reduced[use, owner, block_rows(0), :] = value
+        copies = []
+        for dz in range(1, leaves):
+            here = reduced.at[use, owner, block_rows(0), :]
+            copies.append(
+                send(
+                    here, here, spread_send.at[use, dz], spread_recv.at[use, dz], level(dz)[1]
+                )
+            )
+        for copy in copies:
+            copy.wait_recv()
+        base = leaves
+        first, second = {}, []
+        for d in cross + [sib]:
+            here = reduced.at[use, :, block_rows(0), :]
+            first[d] = send(
+                here, here, spread_send.at[use, base + d], spread_recv.at[use, base + d], peer(d)
+            )
+        for d in cross[::-1]:
+            first[d].wait_recv()
+            here = reduced.at[use, :, block_rows(d), :]
+            second.append(
+                send(
+                    here,
+                    here,
+                    spread_send.at[use, base + d + sib],
+                    spread_recv.at[use, base + d + sib],
+                    peer(sib),
+                )
+            )
+        first[sib].wait_recv()
+        for copy in second:
+            copy.wait_recv()
+
+    def scale_leaf():
+        for c in range(local // step):
+            rows = pl.ds(c * step, step)
+            joined = (
+                doff[:, pl.ds(c * tile_rows, tile_rows)]
+                * pairs[:, pl.ds(c * tile_rows, tile_rows)].astype(f32)
+            )
+            scaled = paired(
+                forward[rows, :].astype(f32), column_of(dinv[:, rows], 1), column_of(joined, 2)
+            )
+            scaled_t[:, rows] = scaled.T
+
+    gathered = sum_all(0, scale_leaf)
+    spread(0, (root_rhs[...].astype(f32) - gathered).astype(bf16))
+    root_load.wait()
+    root_forward = jnp.zeros((root_inv.shape[0], root_rhs.shape[1]), f32)
+    for z in range(leaves):
+        root_forward = root_forward + jnp.dot(
+            root_inv[:, z * band : (z + 1) * band], reduced[0, z], preferred_element_type=f32
+        )
+    root_scaled = paired(
+        root_forward,
+        column_of(root_dinv[...], 1),
+        column_of(root_doff[...] * root_pairs[...].astype(f32), 2),
+    )
+    root_scaled_t = root_scaled.T.astype(bf16)
+    for z in range(leaves):
+        scattered[1, z] = jnp.dot(
+            root_scaled_t, root_inv[:, z * band : (z + 1) * band], preferred_element_type=f32
+        ).T
+    root_own = sum_all(1, lambda: None).astype(bf16)
+    root_out[...] = root_own
+    spread(1, root_own)
+
+    for t in range(leaves * band_tiles):
+        rows = pl.ds(t % band_tiles * tile_rows, tile_rows)
+        whole_t[t] = reduced[1, t // band_tiles, rows, :].astype(f32).T
+    for k in range(tile_count):
+        values_t[:, k * tile_rows : (k + 1) * tile_rows] = whole_t[names[k]].astype(bf16)
+
+    @pl.loop(0, local // step)
+    def _(c):
+        rows = pl.ds(pl.multiple_of(c * step, step), step)
+        coupled = jnp.dot(values_t[...], update[:, rows], preferred_element_type=f32)
+        vector_t[:, rows] = (scaled_t[:, rows] - coupled).astype(bf16)
+
+    def back(d, target):
+        @pl.loop(0, local // step)
+        def _(c):
+            rows = pl.ds(pl.multiple_of(c * step, step), step)
+            target[:, rows] = jnp.dot(
+                vector_t[...], inverse[d, :, rows], preferred_element_type=f32
+            ).astype(target.dtype)
+
+    first, second = {}, {}
+    base = len(spots)
+
+    def pass_on(d):
+        i = spots[d]
+        first[d].wait_recv()
+        back_far_out[i] = (back_keep[i] + back_near_in[i].astype(f32)).astype(bf16)
+        second[d] = send(
+            back_far_out.at[i],
+            back_far_in.at[i],
+            back_send.at[base + i],
+            back_recv.at[base + i],
+            peer(d),
+        )
+
+    previous = None
+    for d in cross + [0]:
+        i = spots[d]
+        back(d + sib, back_near_out.at[i])
+        first[d] = send(
+            back_near_out.at[i], back_near_in.at[i], back_send.at[i], back_recv.at[i], peer(sib)
+        )
+        back(d, back_keep.at[i])
+        if previous is not None:
+            pass_on(previous)
+        previous = d
+    first[0].wait_recv()
+    i = spots[0]
+    result = back_keep[i] + back_near_in[i].astype(f32)
+    for d in cross:
+        second[d].wait_recv()
+        result = result + back_far_in[spots[d]].astype(f32)
+    leaf_out[0] = result.T.astype(bf16)
+    for copy in pending:
+        copy.wait_send()
+
+
+def in_one_kernel(
+    leaf_rhs,
+    leaf_inverse,
+    leaf_update,
+    root_tiles,
+    leaf_dinv,
+    leaf_doff,
+    leaf_pairs,
+    root_rhs,
+    root_inverse,
+    root_dinv,
+    root_doff,
+    root_pairs,
+):
+    f32, bf16 = jnp.float32, jnp.bfloat16
+    leaves, tile_count = root_tiles.shape
+    group_size = lax.axis_size("leaf") // leaves
+    node_count = lax.axis_size("node")
+    members = group_size * node_count
+    local, rhs = leaf_rhs.shape[1:]
+    own_rows, root_rows = root_inverse.shape
+    band = members * own_rows
+    padded = -(-own_rows // tile_rows) * tile_rows
+    half = members // 2
+    dma = pltpu.SemaphoreType.DMA
+    hbm = pl.BlockSpec(memory_space=pl.ANY)
+    vmem = pl.BlockSpec(memory_space=pltpu.VMEM)
+    smem = pl.BlockSpec(memory_space=pltpu.SMEM)
+    flops = 4 * rhs * (local * members * local + tile_count * tile_rows * local)
+    return pl.pallas_call(
+        functools.partial(solve_kernel, leaves, group_size, node_count),
+        out_shape=(
+            jax.ShapeDtypeStruct((1, local, rhs), bf16),
+            jax.ShapeDtypeStruct((own_rows, rhs), bf16),
+        ),
+        in_specs=[hbm, hbm, hbm, smem, vmem, vmem, vmem, vmem, hbm, vmem, vmem, vmem],
+        out_specs=(vmem, vmem),
+        scratch_shapes=[
+            pltpu.VMEM((members, local, rhs), bf16),
+            pltpu.VMEM((members, local, local), bf16),
+            pltpu.VMEM((tile_count * tile_rows, local), bf16),
+            pltpu.VMEM((padded, root_rows), bf16),
+            pltpu.VMEM((local, rhs), f32),
+            pltpu.VMEM((local, rhs), bf16),
+            pltpu.VMEM((tile_count, tile_rows, rhs), f32),
+            pltpu.VMEM((rhs, local), f32),
+            pltpu.VMEM((rhs, local), bf16),
+            pltpu.VMEM((rhs, tile_count * tile_rows), bf16),
+            pltpu.VMEM((root_rows // tile_rows, rhs, tile_rows), f32),
+            pltpu.VMEM((2, leaves, band, rhs), f32),
+            pltpu.VMEM((2, half, leaves, own_rows, rhs), bf16),
+            pltpu.VMEM((2, half, leaves, own_rows, rhs), bf16),
+            pltpu.VMEM((2, half, leaves, own_rows, rhs), bf16),
+            pltpu.VMEM((2, half, leaves, own_rows, rhs), bf16),
+            pltpu.VMEM((2, leaves, own_rows, rhs), bf16),
+            pltpu.VMEM((2, leaves, own_rows, rhs), bf16),
+            pltpu.VMEM((2, leaves, band, rhs), bf16),
+            pltpu.VMEM((half, rhs, local), f32),
+            pltpu.VMEM((half, rhs, local), bf16),
+            pltpu.VMEM((half, rhs, local), bf16),
+            pltpu.VMEM((half, rhs, local), bf16),
+            pltpu.VMEM((half, rhs, local), bf16),
+            dma((members + 3,)),
+            dma((members,)),
+            dma((members,)),
+            dma((2, members + leaves)),
+            dma((2, members + leaves)),
+            dma((2, members + leaves)),
+            dma((2, members + leaves)),
+            dma((members,)),
+            dma((members,)),
+        ],
+        compiler_params=pltpu.CompilerParams(
+            collective_id=0, has_side_effects=True, vmem_limit_bytes=56 * 2**20
+        ),
+        cost_estimate=pl.CostEstimate(
+            flops=flops, bytes_accessed=2 * local * local * members, transcendentals=0
+        ),
+        name="solve",
+    )(
+        leaf_rhs,
+        leaf_inverse,
+        leaf_update,
+        root_tiles,
+        leaf_dinv,
+        leaf_doff,
+        leaf_pairs,
+        root_rhs,
+        root_inverse,
+        root_dinv[None],
+        root_doff[None],
+        root_pairs[None],
+    )
+
+
+def fits_kernel(leaf_rhs, root_tiles, root_rhs, group_size, node_count):
+    members = group_size * node_count
+    local, own_rows = leaf_rhs.shape[1], root_rhs.shape[0]
+    return (
+        group_size > 1
+        and members & (members - 1) == 0
+        and 2 * members * local * local <= 20 * 2**20
+        and leaf_rhs.shape[2] == tile_rows
+        and local % (2 * tile_rows) == 0
+        and own_rows % 16 == 0
+        and members * own_rows % tile_rows == 0
+    )
+
+
+def by_shape(*arrays):
+    leaf_rhs, root_tiles, root_rhs = arrays[0], arrays[3], arrays[7]
+    group_size = lax.axis_size("leaf") // root_tiles.shape[0]
+    if fits_kernel(leaf_rhs, root_tiles, root_rhs, group_size, lax.axis_size("node")):
+        return in_one_kernel(*arrays)
+    return on_device(*arrays)
+
+
 def solution(mesh):
     in_specs = (
         P("leaf", "node", None),
@@ -148,5 +657,5 @@
     )
     out_specs = (P("leaf", "node", None), P(("leaf", "node"), None))
     return jax.shard_map(
-        on_device, mesh=mesh, in_specs=in_specs, out_specs=out_specs, check_vma=False
-    )
+        by_shape, mesh=mesh, in_specs=in_specs, out_specs=out_specs, check_vma=False
+    )

time: 264 us -> 97.7 us (0.37)
  blocking collectives: 123 us -> 0 us
  Pallas kernels: 0 us -> 93.8 us
  waiting for transfers between devices: 54.7 us -> 0 us
  matrix products: 33.7 us -> 0 us
  other arithmetic: 17.7 us -> 0 us
  local copies, waits for them, and re-layouts: 17 us -> 3.02 us
  between operations: 14.3 us -> 0.64 us
  starting transfers between devices: 2.67 us -> 0 us
    psum x2 -> x0, blocking collectives: 111 us -> none  [the longest x1 55.9 us: on_device(): root_full = lax.psum(full_term, ('leaf', 'node')).astype(jnp.bfloat16)]
    pallas_call x0 -> x1, Pallas kernels: none -> 93.8 us  [in_one_kernel(): pl.pallas_call(functools.partial(solve_kernel, leaves, group_size, node_c...]
    ppermute x4 -> x0, waiting for transfers between devices: 42.9 us -> none  [partner(): return lax.ppermute(value, axis, pairs)]
    dot_general x9 -> x0, matrix products: 33.7 us -> none  [the longest x2 13.4 us: transposed_product(): lax.dot_general(matrix, vector, (((0,), (0,)), ((), ())), preferred_eleme...]
    all_gather x1 -> x0, blocking collectives: 12.1 us -> none  [on_device(): holding = lax.all_gather(leaf_rhs[0], 'node', axis=0, tiled=True)]
    reduce_scatter x1 -> x0, waiting for transfers between devices: 11.8 us -> none  [on_device(): lax.psum_scatter(back_term.astype(jnp.bfloat16), 'node', scatter_dimensio...]
    reshape x3 -> x0, local copies, waits for them, and re-layouts: 5.45 us -> none  [the longest x1 2.65 us: on_device(): root_full.reshape(ROOT_TILES, tile_rows, rhs_count)]
    add x2 -> x0, other arithmetic: 5.12 us -> none  [the longest x1 2.9 us: on_device(): keeping + partner(outgoing.astype(jnp.bfloat16), 'leaf', bit_number).asty...]
  transfers between devices with their start and end apart: 5 -> 0, of which waited for: 4 -> 0; matrix products, arithmetic and copies ran while one was open for 4% -> 0% of each run, Pallas kernels for 0% -> 0%
where the time goes in v1:
time: 97.7 us; the launch traced here: 97.4 us
  Pallas kernels  93.8 us (96%)
  local copies, waits for them, and re-layouts  3.02 us (3%)
    pallas_call x1, Pallas kernels, in_one_kernel(): pl.pallas_call(functools.partial(solve_kernel, leaves, group_size, node_c...  93.8 us
    unnamed x2, local copies, waits for them, and re-layouts  3.02 us

profile of v1, /device:TPU:0, one launch (start us, length us, event | category | flops | bytes accessed | tf_op | source)
XLA Modules:
  0.0 97.4 jit_solution(13038795995157107946)
XLA Ops:
  0.6 93.8 %solve.1 = (bf16[1,1024,128]{2,1,0:T(8,128)(2,1)}, bf16[96,128]{1,0:T(8,128)(2,1)}) custom-call(bf16[1,1024,128]{2,1,0:T(8,128)(2,1)} %rhs_hbm.1, bf16[1,1024,8192]{2,1,0:T(8,128)(2,1)} %inverse_hbm.1, bf16[1,1536,1024]{2,1,0:T(8,128)(2,1)} %update_hbm.1, s32[4,12]{1,0:T(4,128)} %tiles.1, f32[1,1024]{1,0:T(1,128)} %dinv.1, f32[1,512]{1,0:T(1,128)} %doff.1, ...), custom_call_target="tpu_custom_call" | custom-call | flops 5100273664 | bytes 16777216 | tf_op jit(solution)/shard_map/solve/pallas_call | solution.py:555
  94.4 1.7 %copy.16 = bf16[1,1024,128]{2,1,0:T(8,128)(2,1)} copy(bf16[1,1024,128]{2,1,0:T(8,128)(2,1)} %get-tuple-element.4) | data formatting | bytes 524288
  96.1 1.3 %copy.17 = bf16[96,128]{1,0:T(8,128)(2,1)} copy(bf16[96,128]{1,0:T(8,128)(2,1)} %get-tuple-element.5) | data formatting | bytes 49152

commit v2 on v1

--- a/solution.py
+++ b/solution.py
@@ -204,6 +204,7 @@
     back_near_in,
     back_far_out,
     back_far_in,
+    back_relay,
     load_sem,
     right_send,
     right_recv,
@@ -249,7 +250,8 @@
         pending.append(copy)
         return copy
 
-    order = [0, sib] + cross[::-1] + [d + sib for d in cross[::-1]]
+    corner, one, two = cross
+    order = [0, sib, one, two, one + sib, two + sib, corner, corner + sib]
     loads = {}
     for d in order:
         start = pl.multiple_of(flipped(member, d) * local, tile_rows)
@@ -280,7 +282,7 @@
     pl.semaphore_wait(barrier, len(near) + leaves - 1)
 
     arrivals = {}
-    for d in cross + [sib]:
+    for d in (one, two, sib):
         arrivals[d] = send(
             rhs_hbm.at[0], right.at[d], right_send.at[d], right_recv.at[d], peer(d)
         )
@@ -300,13 +302,12 @@
                 inverse[d, rows, :], right[d], preferred_element_type=f32
             )
 
-    def relay(d):
-        arrivals[d].wait_recv()
-        arrivals[d + sib] = send(
-            right.at[d],
-            right.at[d + sib],
-            right_send.at[d + sib],
-            right_recv.at[d + sib],
+    def to_sibling(d, rows, slot):
+        return send(
+            right.at[d, rows],
+            right.at[d + sib, rows],
+            right_send.at[slot],
+            right_recv.at[slot],
             peer(sib),
         )
 
@@ -314,15 +315,34 @@
     product(0)
     arrivals[sib].wait_recv()
     product(sib)
-    for d in cross[::-1][:-1]:
-        relay(d)
-    for d in cross[::-1][:-1]:
-        product(d)
-    relay(cross[0])
-    product(cross[0])
-    for d in cross[::-1]:
-        arrivals[d + sib].wait_recv()
-        product(d + sib)
+    halves = [pl.ds(0, local // 2), pl.ds(local // 2, local // 2)]
+    corner_halves = []
+    for d, other, rows, slot in ((one, two, halves[0], corner), (two, one, halves[1], members)):
+        arrivals[d].wait_recv()
+        corner_halves.append(
+            send(
+                right.at[d, rows],
+                right.at[corner, rows],
+                right_send.at[slot],
+                right_recv.at[slot],
+                peer(other),
+            )
+        )
+        arrivals[d + sib] = to_sibling(d, pl.ds(0, local), d + sib)
+    product(one)
+    product(two)
+    arrivals[one + sib].wait_recv()
+    product(one + sib)
+    last = []
+    for copy, rows, slot in zip(corner_halves, halves, (corner + sib, members + 1)):
+        copy.wait_recv()
+        last.append(to_sibling(corner, rows, slot))
+    arrivals[two + sib].wait_recv()
+    product(two + sib)
+    product(corner)
+    for copy in last:
+        copy.wait_recv()
+    product(corner + sib)
     forward[...] = total[...].astype(bf16)
 
     update_load.wait()
@@ -486,38 +506,61 @@
                 vector_t[...], inverse[d, :, rows], preferred_element_type=f32
             ).astype(target.dtype)
 
-    first, second = {}, {}
-    base = len(spots)
-
-    def pass_on(d):
-        i = spots[d]
-        first[d].wait_recv()
-        back_far_out[i] = (back_keep[i] + back_near_in[i].astype(f32)).astype(bf16)
-        second[d] = send(
-            back_far_out.at[i],
-            back_far_in.at[i],
-            back_send.at[base + i],
-            back_recv.at[base + i],
-            peer(d),
-        )
-
-    previous = None
-    for d in cross + [0]:
+    first, later = {}, []
+    lanes = halves
+
+    def to_near(d):
         i = spots[d]
         back(d + sib, back_near_out.at[i])
         first[d] = send(
             back_near_out.at[i], back_near_in.at[i], back_send.at[i], back_recv.at[i], peer(sib)
         )
-        back(d, back_keep.at[i])
-        if previous is not None:
-            pass_on(previous)
-        previous = d
-    first[0].wait_recv()
-    i = spots[0]
-    result = back_keep[i] + back_near_in[i].astype(f32)
-    for d in cross:
-        second[d].wait_recv()
-        result = result + back_far_in[spots[d]].astype(f32)
+
+    def join(d):
+        i = spots[d]
+        first[d].wait_recv()
+        back_keep[i] = back_keep[i] + back_near_in[i].astype(f32)
+
+    def to_far(d, part, target, slot, device):
+        i = spots[d]
+        back_far_out[i, :, lanes[part]] = back_keep[i, :, lanes[part]].astype(bf16)
+        return send(
+            back_far_out.at[i, :, lanes[part]],
+            target,
+            back_send.at[slot],
+            back_recv.at[slot],
+            device,
+        )
+
+    base = len(spots)
+    to_near(corner)
+    back(corner, back_keep.at[spots[corner]])
+    to_near(one)
+    join(corner)
+    relayed = [
+        to_far(corner, 0, back_relay.at[0], base, peer(one)),
+        to_far(corner, 1, back_relay.at[1], base + 1, peer(two)),
+    ]
+    back(one, back_keep.at[spots[one]])
+    to_near(two)
+    join(one)
+    later.append(to_far(one, 0, back_far_in.at[0, :, lanes[0]], base + 2, peer(one)))
+    back(two, back_keep.at[spots[two]])
+    join(two)
+    later.append(to_far(two, 1, back_far_in.at[1, :, lanes[1]], base + 3, peer(two)))
+    for d, part, place in ((two, 0, 1), (one, 1, 0)):
+        i = spots[d]
+        relayed[part].wait_recv()
+        back_keep[i, :, lanes[part]] = back_keep[i, :, lanes[part]] + back_relay[part].astype(f32)
+        later.append(
+            to_far(d, part, back_far_in.at[place, :, lanes[part]], base + 4 + part, peer(d))
+        )
+    to_near(0)
+    back(0, back_keep.at[spots[0]])
+    join(0)
+    for copy in later:
+        copy.wait_recv()
+    result = back_keep[spots[0]] + back_far_in[0].astype(f32) + back_far_in[1].astype(f32)
     leaf_out[0] = result.T.astype(bf16)
     for copy in pending:
         copy.wait_send()
@@ -584,16 +627,17 @@
             pltpu.VMEM((half, rhs, local), bf16),
             pltpu.VMEM((half, rhs, local), bf16),
             pltpu.VMEM((half, rhs, local), bf16),
-            pltpu.VMEM((half, rhs, local), bf16),
+            pltpu.VMEM((2, rhs, local), bf16),
+            pltpu.VMEM((2, rhs, local // 2), bf16),
             dma((members + 3,)),
-            dma((members,)),
-            dma((members,)),
+            dma((members + 2,)),
+            dma((members + 2,)),
             dma((2, members + leaves)),
             dma((2, members + leaves)),
             dma((2, members + leaves)),
             dma((2, members + leaves)),
-            dma((members,)),
-            dma((members,)),
+            dma((members + 2,)),
+            dma((members + 2,)),
         ],
         compiler_params=pltpu.CompilerParams(
             collective_id=0, has_side_effects=True, vmem_limit_bytes=56 * 2**20
@@ -622,8 +666,8 @@
     members = group_size * node_count
     local, own_rows = leaf_rhs.shape[1], root_rhs.shape[0]
     return (
-        group_size > 1
-        and members & (members - 1) == 0
+        group_size % 2 == 0
+        and members == 8
         and 2 * members * local * local <= 20 * 2**20
         and leaf_rhs.shape[2] == tile_rows
         and local % (2 * tile_rows) == 0

time: 97.7 us -> 89.3 us (0.914)
  Pallas kernels: 93.8 us -> 85.4 us
    pallas_call x1, Pallas kernels: 93.8 us -> 85.4 us  [in_one_kernel(): pl.pallas_call(functools.partial(solve_kernel, leaves, group_size, node_c...]
where the time goes in v2:
time: 89.3 us; the launch traced here: 89.1 us
  Pallas kernels  85.4 us (96%)
  local copies, waits for them, and re-layouts  3.02 us (3%)
    pallas_call x1, Pallas kernels, in_one_kernel(): pl.pallas_call(functools.partial(solve_kernel, leaves, group_size, node_c...  85.4 us
    unnamed x2, local copies, waits for them, and re-layouts  3.02 us

profile of v2, /device:TPU:0, one launch (start us, length us, event | category | flops | bytes accessed | tf_op | source)
XLA Modules:
  0.0 89.1 jit_solution(9590577861913888034)
XLA Ops:
  0.6 85.4 %solve.1 = (bf16[1,1024,128]{2,1,0:T(8,128)(2,1)}, bf16[96,128]{1,0:T(8,128)(2,1)}) custom-call(bf16[1,1024,128]{2,1,0:T(8,128)(2,1)} %rhs_hbm.1, bf16[1,1024,8192]{2,1,0:T(8,128)(2,1)} %inverse_hbm.1, bf16[1,1536,1024]{2,1,0:T(8,128)(2,1)} %update_hbm.1, s32[4,12]{1,0:T(4,128)} %tiles.1, f32[1,1024]{1,0:T(1,128)} %dinv.1, f32[1,512]{1,0:T(1,128)} %doff.1, ...), custom_call_target="tpu_custom_call" | custom-call | flops 5100273664 | bytes 16777216 | tf_op jit(solution)/shard_map/solve/pallas_call | solution.py:598
  86.1 1.7 %copy.16 = bf16[1,1024,128]{2,1,0:T(8,128)(2,1)} copy(bf16[1,1024,128]{2,1,0:T(8,128)(2,1)} %get-tuple-element.4) | data formatting | bytes 524288
  87.7 1.3 %copy.17 = bf16[96,128]{1,0:T(8,128)(2,1)} copy(bf16[96,128]{1,0:T(8,128)(2,1)} %get-tuple-element.5) | data formatting | bytes 49152

commit v3 on v2

--- a/solution.py
+++ b/solution.py
@@ -178,8 +178,7 @@
     root_dinv,
     root_doff,
     root_pairs,
-    leaf_out,
-    root_out,
+    out,
     right,
     inverse,
     update,
@@ -295,9 +294,9 @@
     def product(d):
         loads[d].wait()
 
-        @pl.loop(0, local // step)
+        @pl.loop(0, 2)
         def _(i):
-            rows = pl.ds(pl.multiple_of(i * step, step), step)
+            rows = pl.ds(pl.multiple_of(i * (local // 2), tile_rows), local // 2)
             total[rows, :] += jnp.dot(
                 inverse[d, rows, :], right[d], preferred_element_type=f32
             )
@@ -348,10 +347,14 @@
     update_load.wait()
     tile_count = update.shape[0] // tile_rows
 
-    @pl.loop(0, tile_count)
+    batch = 4 if tile_count % 4 == 0 else 1
+
+    @pl.loop(0, tile_count // batch)
     def _(k):
-        rows = pl.ds(pl.multiple_of(k * tile_rows, tile_rows), tile_rows)
-        term[k] = jnp.dot(update[rows, :], forward[...], preferred_element_type=f32)
+        length = batch * tile_rows
+        rows = pl.ds(pl.multiple_of(k * length, length), length)
+        product_rows = jnp.dot(update[rows, :], forward[...], preferred_element_type=f32)
+        term[pl.ds(k * batch, batch)] = product_rows.reshape(batch, *term.shape[1:])
 
     names = [tiles[owner, k] for k in range(tile_count)]
     for t in range(leaves * band_tiles):
@@ -379,76 +382,80 @@
                 peer(sib),
             )
         base = len(spots)
+        turns = list(range(1, leaves)) + [0]
         for d in cross:
             i = spots[d]
             first[d].wait_recv()
             both = scattered[use, :, block_rows(d), :] + near_in[use, i].astype(f32)
             far_out[use, i] = both.astype(bf16)
-            second[d] = send(
-                far_out.at[use, i],
-                far_in.at[use, i],
-                sum_send.at[use, base + i],
-                sum_recv.at[use, base + i],
-                peer(d),
-            )
+            for dz in turns:
+                other = level(dz)[0]
+                slot = base + i * leaves + dz
+                second[d, dz] = send(
+                    far_out.at[use, i, other],
+                    far_in.at[use, i, other],
+                    sum_send.at[use, slot],
+                    sum_recv.at[use, slot],
+                    peer(d),
+                )
         meanwhile()
         first[0].wait_recv()
-        mine = scattered[use, :, block_rows(0), :] + near_in[use, spots[0]].astype(f32)
-        for d in cross:
-            second[d].wait_recv()
-            mine = mine + far_in[use, spots[d]].astype(f32)
-        deep_out[use] = mine.astype(bf16)
-        base += len(cross)
+        base += len(cross) * leaves
         third = []
-        for dz in range(1, leaves):
+        for dz in turns:
             other, device = level(dz)
-            third.append(
-                send(
-                    deep_out.at[use, other],
-                    deep_in.at[use, dz],
-                    sum_send.at[use, base + dz],
-                    sum_recv.at[use, base + dz],
-                    device,
+            mine = scattered[use, other, block_rows(0), :]
+            mine = mine + near_in[use, spots[0], other].astype(f32)
+            for d in cross:
+                second[d, dz].wait_recv()
+                mine = mine + far_in[use, spots[d], other].astype(f32)
+            if dz:
+                deep_out[use, dz] = mine.astype(bf16)
+                third.append(
+                    send(
+                        deep_out.at[use, dz],
+                        deep_in.at[use, dz],
+                        sum_send.at[use, base + dz],
+                        sum_recv.at[use, base + dz],
+                        device,
+                    )
                 )
-            )
-        result = deep_out[use, owner].astype(f32)
         for dz in range(1, leaves):
             third[dz - 1].wait_recv()
-            result = result + deep_in[use, dz].astype(f32)
-        return result
+            mine = mine + deep_in[use, dz].astype(f32)
+        return mine
 
     def spread(use, value):
         reduced[use, owner, block_rows(0), :] = value
-        copies = []
+        copies = {}
         for dz in range(1, leaves):
             here = reduced.at[use, owner, block_rows(0), :]
-            copies.append(
-                send(
-                    here, here, spread_send.at[use, dz], spread_recv.at[use, dz], level(dz)[1]
+            copies[dz] = send(
+                here, here, spread_send.at[use, dz], spread_recv.at[use, dz], level(dz)[1]
+            )
+        first, second = {}, []
+        for dz in range(leaves):
+            if dz:
+                copies[dz].wait_recv()
+            source = lax.rem(owner + leaves - dz, leaves)
+            for i, d in enumerate(cross + [sib]):
+                here = reduced.at[use, source, block_rows(0), :]
+                slot = leaves * (i + 1) + dz
+                first[d, dz] = send(
+                    here, here, spread_send.at[use, slot], spread_recv.at[use, slot], peer(d)
                 )
-            )
-        for copy in copies:
-            copy.wait_recv()
-        base = leaves
-        first, second = {}, []
-        for d in cross + [sib]:
-            here = reduced.at[use, :, block_rows(0), :]
-            first[d] = send(
-                here, here, spread_send.at[use, base + d], spread_recv.at[use, base + d], peer(d)
-            )
-        for d in cross[::-1]:
-            first[d].wait_recv()
+        base = leaves * (len(cross) + 2)
+        for i, d in enumerate(cross):
+            for dz in range(leaves):
+                first[d, dz].wait_recv()
             here = reduced.at[use, :, block_rows(d), :]
             second.append(
                 send(
-                    here,
-                    here,
-                    spread_send.at[use, base + d + sib],
-                    spread_recv.at[use, base + d + sib],
-                    peer(sib),
+                    here, here, spread_send.at[use, base + i], spread_recv.at[use, base + i], peer(sib)
                 )
             )
-        first[sib].wait_recv()
+        for dz in range(leaves):
+            first[sib, dz].wait_recv()
         for copy in second:
             copy.wait_recv()
 
@@ -483,7 +490,7 @@
             root_scaled_t, root_inv[:, z * band : (z + 1) * band], preferred_element_type=f32
         ).T
     root_own = sum_all(1, lambda: None).astype(bf16)
-    root_out[...] = root_own
+    out[pl.ds(local, own_rows), :] = root_own
     spread(1, root_own)
 
     for t in range(leaves * band_tiles):
@@ -561,7 +568,7 @@
     for copy in later:
         copy.wait_recv()
     result = back_keep[spots[0]] + back_far_in[0].astype(f32) + back_far_in[1].astype(f32)
-    leaf_out[0] = result.T.astype(bf16)
+    out[pl.ds(0, local), :] = result.T.astype(bf16)
     for copy in pending:
         copy.wait_send()
 
@@ -595,14 +602,11 @@
     vmem = pl.BlockSpec(memory_space=pltpu.VMEM)
     smem = pl.BlockSpec(memory_space=pltpu.SMEM)
     flops = 4 * rhs * (local * members * local + tile_count * tile_rows * local)
-    return pl.pallas_call(
+    both = pl.pallas_call(
         functools.partial(solve_kernel, leaves, group_size, node_count),
-        out_shape=(
-            jax.ShapeDtypeStruct((1, local, rhs), bf16),
-            jax.ShapeDtypeStruct((own_rows, rhs), bf16),
-        ),
+        out_shape=jax.ShapeDtypeStruct((local + own_rows, rhs), bf16),
         in_specs=[hbm, hbm, hbm, smem, vmem, vmem, vmem, vmem, hbm, vmem, vmem, vmem],
-        out_specs=(vmem, vmem),
+        out_specs=vmem,
         scratch_shapes=[
             pltpu.VMEM((members, local, rhs), bf16),
             pltpu.VMEM((members, local, local), bf16),
@@ -632,10 +636,10 @@
             dma((members + 3,)),
             dma((members + 2,)),
             dma((members + 2,)),
-            dma((2, members + leaves)),
-            dma((2, members + leaves)),
-            dma((2, members + leaves)),
-            dma((2, members + leaves)),
+            dma((2, leaves * (half + 2))),
+            dma((2, leaves * (half + 2))),
+            dma((2, leaves * (half + 2))),
+            dma((2, leaves * (half + 2))),
             dma((members + 2,)),
             dma((members + 2,)),
         ],
@@ -660,6 +664,7 @@
         root_doff[None],
         root_pairs[None],
     )
+    return both[None, :local], both[local:]
 
 
 def fits_kernel(leaf_rhs, root_tiles, root_rhs, group_size, node_count):

time: 89.3 us -> 86.2 us (0.965)
  Pallas kernels: 85.4 us -> 82.3 us
    pallas_call x1, Pallas kernels: 85.4 us -> 82.3 us  [in_one_kernel(): pl.pallas_call(functools.partial(solve_kernel, leaves, group_size, node_c...]
    unnamed x2 -> x0, local copies, waits for them, and re-layouts: 3.02 us -> none
    broadcast_in_dim x0 -> x1, local copies, waits for them, and re-layouts: none -> 1.67 us  [in_one_kernel(): return (both[None, :local], both[local:])]
    slice x0 -> x1, local copies, waits for them, and re-layouts: none -> 1.35 us  [in_one_kernel(): return (both[None, :local], both[local:])]
where the time goes in v3:
time: 86.2 us; the launch traced here: 86 us
  Pallas kernels  82.3 us (95%)
  local copies, waits for them, and re-layouts  3.02 us (4%)
    pallas_call x1, Pallas kernels, in_one_kernel(): pl.pallas_call(functools.partial(solve_kernel, leaves, group_size, node_c...  82.3 us

profile of v3, /device:TPU:0, one launch (start us, length us, event | category | flops | bytes accessed | tf_op | source)
XLA Modules:
  0.0 86.0 jit_solution(1088773248475092036)
XLA Ops:
  0.6 82.3 %solve.1 = bf16[1120,128]{1,0:T(8,128)(2,1)} custom-call(bf16[1,1024,128]{2,1,0:T(8,128)(2,1)} %rhs_hbm.1, bf16[1,1024,8192]{2,1,0:T(8,128)(2,1)} %inverse_hbm.1, bf16[1,1536,1024]{2,1,0:T(8,128)(2,1)} %update_hbm.1, s32[4,12]{1,0:T(4,128)} %tiles.1, f32[1,1024]{1,0:T(1,128)} %dinv.1, f32[1,512]{1,0:T(1,128)} %doff.1, s32[1,512]{1,0:T(1,128)} %pairs.1, ...), custom_call_target="tpu_custom_call" | custom-call | flops 5100273664 | bytes 16777216 | tf_op jit(solution)/shard_map/solve/pallas_call | solution.py:605
  83.0 1.3 %slice.7 = bf16[96,128]{1,0:T(8,128)(2,1)} slice(bf16[1120,128]{1,0:T(8,128)(2,1)} %solve.1), slice={[1024:1120], [0:128]} | slice | bytes 49152 | tf_op jit(solution)/shard_map/slice | solution.py:667
  84.3 1.7 %slice_bitcast_fusion = bf16[1,1024,128]{2,1,0:T(8,128)(2,1)} fusion(bf16[1120,128]{1,0:T(8,128)(2,1)} %solve.1), kind=kLoop, calls=%fused_computation | loop fusion | bytes 524288 | tf_op jit(solution)/shard_map/broadcast_in_dim | solution.py:667

commit v4 on v3

--- a/solution.py
+++ b/solution.py
@@ -189,7 +189,7 @@
     scaled_t,
     vector_t,
     values_t,
-    whole_t,
+    whole,
     scattered,
     near_out,
     near_in,
@@ -280,11 +280,23 @@
         )
     pl.semaphore_wait(barrier, len(near) + leaves - 1)
 
-    arrivals = {}
-    for d in (one, two, sib):
-        arrivals[d] = send(
-            rhs_hbm.at[0], right.at[d], right_send.at[d], right_recv.at[d], peer(d)
-        )
+    halves = [pl.ds(0, local // 2), pl.ds(local // 2, local // 2)]
+    arrivals, late = {}, {}
+
+    def own_half(d, rows, slot):
+        return send(
+            rhs_hbm.at[0, rows],
+            right.at[d, rows],
+            right_send.at[slot],
+            right_recv.at[slot],
+            peer(d),
+        )
+
+    arrivals[one] = own_half(one, halves[0], one)
+    arrivals[two] = own_half(two, halves[1], two)
+    arrivals[sib] = own_half(sib, pl.ds(0, local), sib)
+    late[one] = own_half(one, halves[1], members + 2)
+    late[two] = own_half(two, halves[0], members + 3)
     total[...] = jnp.zeros_like(total)
     if root_inv.shape[0] > own_rows:
         root_inv[own_rows:, :] = jnp.zeros(
@@ -314,7 +326,6 @@
     product(0)
     arrivals[sib].wait_recv()
     product(sib)
-    halves = [pl.ds(0, local // 2), pl.ds(local // 2, local // 2)]
     corner_halves = []
     for d, other, rows, slot in ((one, two, halves[0], corner), (two, one, halves[1], members)):
         arrivals[d].wait_recv()
@@ -327,6 +338,8 @@
                 peer(other),
             )
         )
+    for d in (one, two):
+        late[d].wait_recv()
         arrivals[d + sib] = to_sibling(d, pl.ds(0, local), d + sib)
     product(one)
     product(two)
@@ -470,7 +483,10 @@
                 forward[rows, :].astype(f32), column_of(dinv[:, rows], 1), column_of(joined, 2)
             )
             scaled_t[:, rows] = scaled.T
-
+        columns.append(column_of(root_dinv[...], 1))
+        columns.append(column_of(root_doff[...] * root_pairs[...].astype(f32), 2))
+
+    columns = []
     gathered = sum_all(0, scale_leaf)
     spread(0, (root_rhs[...].astype(f32) - gathered).astype(bf16))
     root_load.wait()
@@ -479,11 +495,7 @@
         root_forward = root_forward + jnp.dot(
             root_inv[:, z * band : (z + 1) * band], reduced[0, z], preferred_element_type=f32
         )
-    root_scaled = paired(
-        root_forward,
-        column_of(root_dinv[...], 1),
-        column_of(root_doff[...] * root_pairs[...].astype(f32), 2),
-    )
+    root_scaled = paired(root_forward, *columns)
     root_scaled_t = root_scaled.T.astype(bf16)
     for z in range(leaves):
         scattered[1, z] = jnp.dot(
@@ -495,9 +507,9 @@
 
     for t in range(leaves * band_tiles):
         rows = pl.ds(t % band_tiles * tile_rows, tile_rows)
-        whole_t[t] = reduced[1, t // band_tiles, rows, :].astype(f32).T
+        whole[t] = reduced[1, t // band_tiles, rows, :].astype(f32)
     for k in range(tile_count):
-        values_t[:, k * tile_rows : (k + 1) * tile_rows] = whole_t[names[k]].astype(bf16)
+        values_t[:, k * tile_rows : (k + 1) * tile_rows] = whole[names[k]].T.astype(bf16)
 
     @pl.loop(0, local // step)
     def _(c):
@@ -505,8 +517,11 @@
         coupled = jnp.dot(values_t[...], update[:, rows], preferred_element_type=f32)
         vector_t[:, rows] = (scaled_t[:, rows] - coupled).astype(bf16)
 
-    def back(d, target):
-        @pl.loop(0, local // step)
+    def back(d, target, part=None):
+        steps = local // step
+        start, stop = (0, steps) if part is None else (part * steps // 2, (part + 1) * steps // 2)
+
+        @pl.loop(start, stop)
         def _(c):
             rows = pl.ds(pl.multiple_of(c * step, step), step)
             target[:, rows] = jnp.dot(
@@ -540,14 +555,36 @@
         )
 
     base = len(spots)
-    to_near(corner)
-    back(corner, back_keep.at[spots[corner]])
+    i = spots[corner]
+    corner_near, relayed = [], []
+
+    def corner_near_half(part):
+        back(corner + sib, back_near_out.at[i], part)
+        slot = i if part == 0 else base + 6
+        corner_near.append(
+            send(
+                back_near_out.at[i, :, lanes[part]],
+                back_near_in.at[i, :, lanes[part]],
+                back_send.at[slot],
+                back_recv.at[slot],
+                peer(sib),
+            )
+        )
+
+    def corner_far_half(part, device):
+        corner_near[part].wait_recv()
+        back_keep[i, :, lanes[part]] = back_keep[i, :, lanes[part]] + back_near_in[
+            i, :, lanes[part]
+        ].astype(f32)
+        relayed.append(to_far(corner, part, back_relay.at[part], base + part, device))
+
+    corner_near_half(0)
+    back(corner, back_keep.at[i], 0)
+    corner_near_half(1)
+    corner_far_half(0, peer(one))
+    back(corner, back_keep.at[i], 1)
     to_near(one)
-    join(corner)
-    relayed = [
-        to_far(corner, 0, back_relay.at[0], base, peer(one)),
-        to_far(corner, 1, back_relay.at[1], base + 1, peer(two)),
-    ]
+    corner_far_half(1, peer(two))
     back(one, back_keep.at[spots[one]])
     to_near(two)
     join(one)
@@ -634,14 +671,14 @@
             pltpu.VMEM((2, rhs, local), bf16),
             pltpu.VMEM((2, rhs, local // 2), bf16),
             dma((members + 3,)),
-            dma((members + 2,)),
-            dma((members + 2,)),
+            dma((members + 4,)),
+            dma((members + 4,)),
             dma((2, leaves * (half + 2))),
             dma((2, leaves * (half + 2))),
             dma((2, leaves * (half + 2))),
             dma((2, leaves * (half + 2))),
-            dma((members + 2,)),
-            dma((members + 2,)),
+            dma((members + 3,)),
+            dma((members + 3,)),
         ],
         compiler_params=pltpu.CompilerParams(
             collective_id=0, has_side_effects=True, vmem_limit_bytes=56 * 2**20

time: 86.2 us -> 86.5 us (level)
  no operation moved by 1% of the time
where the time goes in v4:
time: 86.5 us; the launch traced here: 86.3 us
  Pallas kernels  82.6 us (95%)
  local copies, waits for them, and re-layouts  3.02 us (3%)
    pallas_call x1, Pallas kernels, in_one_kernel(): pl.pallas_call(functools.partial(solve_kernel, leaves, group_size, node_c...  82.6 us

profile of v4, /device:TPU:0, one launch (start us, length us, event | category | flops | bytes accessed | tf_op | source)
XLA Modules:
  0.0 86.3 jit_solution(7635296157575435836)
XLA Ops:
  0.6 82.6 %solve.1 = bf16[1120,128]{1,0:T(8,128)(2,1)} custom-call(bf16[1,1024,128]{2,1,0:T(8,128)(2,1)} %rhs_hbm.1, bf16[1,1024,8192]{2,1,0:T(8,128)(2,1)} %inverse_hbm.1, bf16[1,1536,1024]{2,1,0:T(8,128)(2,1)} %update_hbm.1, s32[4,12]{1,0:T(4,128)} %tiles.1, f32[1,1024]{1,0:T(1,128)} %dinv.1, f32[1,512]{1,0:T(1,128)} %doff.1, s32[1,512]{1,0:T(1,128)} %pairs.1, ...), custom_call_target="tpu_custom_call" | custom-call | flops 5100273664 | bytes 16777216 | tf_op jit(solution)/shard_map/solve/pallas_call | solution.py:642
  83.3 1.3 %slice.7 = bf16[96,128]{1,0:T(8,128)(2,1)} slice(bf16[1120,128]{1,0:T(8,128)(2,1)} %solve.1), slice={[1024:1120], [0:128]} | slice | bytes 49152 | tf_op jit(solution)/shard_map/slice | solution.py:704
  84.6 1.7 %slice_bitcast_fusion = bf16[1,1024,128]{2,1,0:T(8,128)(2,1)} fusion(bf16[1120,128]{1,0:T(8,128)(2,1)} %solve.1), kind=kLoop, calls=%fused_computation | loop fusion | bytes 524288 | tf_op jit(solution)/shard_map/broadcast_in_dim | solution.py:704

commit v5 on v4

--- a/solution.py
+++ b/solution.py
@@ -306,12 +306,7 @@
     def product(d):
         loads[d].wait()
 
-        @pl.loop(0, 2)
-        def _(i):
-            rows = pl.ds(pl.multiple_of(i * (local // 2), tile_rows), local // 2)
-            total[rows, :] += jnp.dot(
-                inverse[d, rows, :], right[d], preferred_element_type=f32
-            )
+        total[...] += jnp.dot(inverse[d], right[d], preferred_element_type=f32)
 
     def to_sibling(d, rows, slot):
         return send(
@@ -360,7 +355,7 @@
     update_load.wait()
     tile_count = update.shape[0] // tile_rows
 
-    batch = 4 if tile_count % 4 == 0 else 1
+    batch = tile_count // 2 if tile_count % 2 == 0 else 1
 
     @pl.loop(0, tile_count // batch)
     def _(k):

time: 86.5 us -> 88 us (1.017)
  Pallas kernels: 82.6 us -> 84.1 us
    pallas_call x1, Pallas kernels: 82.6 us -> 84.1 us  [in_one_kernel(): pl.pallas_call(functools.partial(solve_kernel, leaves, group_size, node_c...]
where the time goes in v5:
time: 88 us; the launch traced here: 87.8 us
  Pallas kernels  84.1 us (96%)
  local copies, waits for them, and re-layouts  3.02 us (3%)
    pallas_call x1, Pallas kernels, in_one_kernel(): pl.pallas_call(functools.partial(solve_kernel, leaves, group_size, node_c...  84.1 us

profile of v5, /device:TPU:0, one launch (start us, length us, event | category | flops | bytes accessed | tf_op | source)
XLA Modules:
  0.0 87.8 jit_solution(10435035637906932721)
XLA Ops:
  0.6 84.1 %solve.1 = bf16[1120,128]{1,0:T(8,128)(2,1)} custom-call(bf16[1,1024,128]{2,1,0:T(8,128)(2,1)} %rhs_hbm.1, bf16[1,1024,8192]{2,1,0:T(8,128)(2,1)} %inverse_hbm.1, bf16[1,1536,1024]{2,1,0:T(8,128)(2,1)} %update_hbm.1, s32[4,12]{1,0:T(4,128)} %tiles.1, f32[1,1024]{1,0:T(1,128)} %dinv.1, f32[1,512]{1,0:T(1,128)} %doff.1, s32[1,512]{1,0:T(1,128)} %pairs.1, ...), custom_call_target="tpu_custom_call" | custom-call | flops 5100273664 | bytes 16777216 | tf_op jit(solution)/shard_map/solve/pallas_call | solution.py:637
  84.7 1.3 %slice.7 = bf16[96,128]{1,0:T(8,128)(2,1)} slice(bf16[1120,128]{1,0:T(8,128)(2,1)} %solve.1), slice={[1024:1120], [0:128]} | slice | bytes 49152 | tf_op jit(solution)/shard_map/slice | solution.py:699
  86.1 1.7 %slice_bitcast_fusion = bf16[1,1024,128]{2,1,0:T(8,128)(2,1)} fusion(bf16[1120,128]{1,0:T(8,128)(2,1)} %solve.1), kind=kLoop, calls=%fused_computation | loop fusion | bytes 524288 | tf_op jit(solution)/shard_map/broadcast_in_dim | solution.py:699
